TPU v7x, 256 devices: a whole 4x4x8 slice. The times are simulated.
256 devices in a mesh: row: 16 (over y, z_hi, core), col: 16 (over x, z_lo).
Axes of the slice: x: 4, y: 4, z: 8 (z_hi: 2, z_lo: 4; z = z_hi * 4 + z_lo), core: 2. Of those that a mesh axis runs over, the one named last changes fastest.
Arguments:
- images: bfloat16 [196608, 1152], P(('row', 'col')), may hold values from -6 to 6
- texts: bfloat16 [196608, 1152], P(('row', 'col')), may hold values from -6 to 6
- logit_scale: float32 [1], replicated, may hold values from 0.01 to 0.03
- logit_bias: float32 [1], replicated, may hold values from -2 to -0.5
Outputs:
- image_grad: bfloat16 [196608, 1152], P(('row', 'col'))
- text_grad: bfloat16 [196608, 1152], P(('row', 'col'))
All inputs are finite; a program needn't handle non-finite values.
Results may differ from a plain program's by a relative error of at most 0.0042.
Values may be sent and summed in bfloat16 or wider, within the bound.
A program may use at most 64 MiB of HBM per device.

v0:
```python
import jax
import jax.numpy as jnp
from jax import lax
from jax.sharding import PartitionSpec as P


def partner(block, axis, bit):
    count = lax.axis_size(axis)
    route = []
    for low in range(count):
        high = low | 1 << bit
        if high != low and high < count:
            route += [(low, high), (high, low)]
    return lax.ppermute(block, axis, route)


def block_grad(left, right, scale, bias, positive):
    logits = (
        lax.dot_general(left, right, (((1,), (1,)), ((), ())), preferred_element_type=jnp.float32)
        * scale
        + bias
    )
    eye_mask = jnp.eye(left.shape[0], dtype=jnp.float32) * positive
    return (jax.nn.sigmoid(logits) - eye_mask).astype(jnp.bfloat16)


def image_term(grad, right, scale):
    return scale * jnp.dot(grad, right, preferred_element_type=jnp.float32)


def text_term(grad, left, scale):
    return scale * lax.dot_general(
        grad, left, (((0,), (0,)), ((), ())), preferred_element_type=jnp.float32
    )


def shards(images, texts, logit_scale, logit_bias):
    scale = logit_scale[0]
    bias = logit_bias[0]
    row_bits = lax.axis_size("row").bit_length() - 1
    col_bits = lax.axis_size("col").bit_length() - 1
    rounds_bits = [col_bits + row_bits - 1, col_bits - 1]
    own = block_grad(images, texts, scale, bias, 1.0)
    image_acc = image_term(own, texts, scale)
    text_acc = text_term(own, images, scale)
    for bit in rounds_bits:
        partner_texts = partner(texts, ("row", "col"), bit)
        grad = block_grad(images, partner_texts, scale, bias, 0.0)
        image_acc = image_acc + image_term(grad, partner_texts, scale)
        partial_value = text_term(grad, images, scale)
        text_acc = text_acc + partner(partial_value, ("row", "col"), bit)
    return (image_acc.astype(jnp.bfloat16), text_acc.astype(jnp.bfloat16))


def solution(mesh):
    placed = (P(("row", "col"), None), P(("row", "col"), None), P(), P())
    return jax.shard_map(
        shards,
        mesh=mesh,
        in_specs=placed,
        out_specs=(P(("row", "col"), None), P(("row", "col"), None)),
        check_vma=False,
    )
```

profile of v0, /device:TPU:160, one launch (start us, length us, event | category | flops | bytes accessed | tf_op | source)
XLA Modules:
  0.0 135.2 jit_solution(15481021447945341071)
XLA Ops:
  0.6 0.0 copy-start
  0.6 3.1 %collective-permute-start.1 = (bf16[768,1152]{1,0:T(8,128)(2,1)}, bf16[768,1152]{1,0:T(8,128)(2,1)S(1)}, u32[]{:S(2)}, u32[]{:S(2)}) collective-permute-start(bf16[768,1152]{1,0:T(8,128)(2,1)} %param.5), channel_id=1, source_target_pairs={{0,8},{8,0},{1,9},{9,1},{2,10},{10,2},{3,11},{11,3},{4,12},{12,4},... | collective-permute-start | bytes 5308424 | tf_op jit(solution)/shard_map/ppermute | solution.py:14
  3.8 3.2 %collective-permute-start = (bf16[768,1152]{1,0:T(8,128)(2,1)}, bf16[768,1152]{1,0:T(8,128)(2,1)S(1)}, u32[]{:S(2)}, u32[]{:S(2)}) collective-permute-start(bf16[768,1152]{1,0:T(8,128)(2,1)} %param.5), channel_id=1, source_target_pairs={{0,128},{128,0},{1,129},{129,1},{2,130},{130,2},{3,131},{131,3},{4... | collective-permute-start | bytes 5308424 | tf_op jit(solution)/shard_map/ppermute | solution.py:14
  8.2 34.5 %collective-permute-done.1 = bf16[768,1152]{1,0:T(8,128)(2,1)S(1)} collective-permute-done((bf16[768,1152]{1,0:T(8,128)(2,1)}, bf16[768,1152]{1,0:T(8,128)(2,1)S(1)}, u32[]{:S(2)}, u32[]{:S(2)}) %collective-permute-start.1) | collective-permute-done | bytes 1769504 | tf_op jit(solution)/shard_map/ppermute | solution.py:14
  42.8 0.0 copy-done
  42.8 1.9 %divide_convert_fusion = bf16[768,768]{1,0:T(8,128)(2,1)S(1)} fusion(bf16[768,1152]{1,0:T(8,128)(2,1)S(1)} %copy-done, bf16[768,1152]{1,0:T(8,128)(2,1)S(1)} %collective-permute-done.1, f32[]{:T(128)} %bitcast.28, f32[]{:T(128)} %bitcast.25), kind=kOutput, calls=%fused_computation.10 | convolution fusion | flops 1362493440 | bytes 4718600 | tf_op jit(solution)/shard_map/dot_general | solution.py:19
  44.7 1.7 %convolution_multiply_fusion = f32[768,1152]{1,0:T(8,128)S(1)} fusion(bf16[768,768]{1,0:T(8,128)(2,1)S(1)} %divide_convert_fusion, bf16[768,1152]{1,0:T(8,128)(2,1)S(1)} %copy-done, f32[]{:T(128)} %bitcast.24), kind=kOutput, calls=%fused_computation | convolution fusion | flops 1359839232 | bytes 6488068 | tf_op jit(solution)/shard_map/dot_general | solution.py:32
  46.5 3.1 %collective-permute-start.3 = (f32[768,1152]{1,0:T(8,128)S(1)}, f32[768,1152]{1,0:T(8,128)S(1)}, u32[]{:S(2)}, u32[]{:S(2)}) collective-permute-start(f32[768,1152]{1,0:T(8,128)S(1)} %convolution_multiply_fusion), channel_id=1, source_target_pairs={{0,8},{8,0},{1,9},{9,1},{2,10},{10,2},{3,11},{11,3},{4,12},{12,4},... | collective-permute-start | bytes 10616840 | tf_op jit(solution)/shard_map/ppermute | solution.py:14
  49.6 0.0 collective-permute-done
  49.6 1.9 %divide_convert_fusion.1 = bf16[768,768]{1,0:T(8,128)(2,1)S(1)} fusion(bf16[768,1152]{1,0:T(8,128)(2,1)S(1)} %copy-done, bf16[768,1152]{1,0:T(8,128)(2,1)S(1)} %collective-permute-done, f32[]{:T(128)} %bitcast.29, f32[]{:T(128)} %bitcast.26), kind=kOutput, calls=%fused_computation.11 | convolution fusion | flops 1362493440 | bytes 4718600 | tf_op jit(solution)/shard_map/dot_general | solution.py:19
  51.6 0.0 copy-start.1
  51.6 1.7 %convolution_multiply_fusion.1 = f32[768,1152]{1,0:T(8,128)S(1)} fusion(bf16[768,768]{1,0:T(8,128)(2,1)S(1)} %divide_convert_fusion.1, bf16[768,1152]{1,0:T(8,128)(2,1)S(1)} %copy-done, f32[]{:T(128)} %bitcast.23), kind=kOutput, calls=%fused_computation.1 | convolution fusion | flops 1359839232 | bytes 6488068 | tf_op jit(solution)/shard_map/dot_general | solution.py:32
  53.3 3.4 %collective-permute-start.2 = (f32[768,1152]{1,0:T(8,128)S(1)}, f32[768,1152]{1,0:T(8,128)S(1)}, u32[]{:S(2)}, u32[]{:S(2)}) collective-permute-start(f32[768,1152]{1,0:T(8,128)S(1)} %convolution_multiply_fusion.1), channel_id=1, source_target_pairs={{0,128},{128,0},{1,129},{129,1},{2,130},{130,2},{3,131},{131,3},{4... | collective-permute-start | bytes 10616840 | tf_op jit(solution)/shard_map/ppermute | solution.py:14
  56.8 0.0 copy-done.1
  56.8 1.9 %subtract_convert_fusion = bf16[768,768]{1,0:T(8,128)(2,1)S(1)} fusion(bf16[768,1152]{1,0:T(8,128)(2,1)S(1)} %copy-done, bf16[768,1152]{1,0:T(8,128)(2,1)S(1)} %copy-done.1, f32[]{:T(128)} %bitcast.27, f32[]{:T(128)} %bitcast.21), kind=kOutput, calls=%fused_computation.12 | convolution fusion | flops 1364262912 | bytes 4718600 | tf_op jit(solution)/shard_map/dot_general | solution.py:19
  58.7 1.7 %fusion.5 = f32[768,1152]{1,0:T(8,128)S(1)} fusion(bf16[768,768]{1,0:T(8,128)(2,1)S(1)} %subtract_convert_fusion, bf16[768,1152]{1,0:T(8,128)(2,1)S(1)} %copy-done.1), kind=kOutput, calls=%fused_computation.14 | convolution fusion | flops 1358954496 | bytes 6488064 | tf_op jit(solution)/shard_map/dot_general | solution.py:28
  60.4 1.8 %convolution_add_fusion.1 = f32[768,1152]{1,0:T(8,128)S(1)} fusion(f32[768,1152]{1,0:T(8,128)S(1)} %fusion.5, bf16[768,768]{1,0:T(8,128)(2,1)S(1)} %divide_convert_fusion.1, bf16[768,1152]{1,0:T(8,128)(2,1)S(1)} %collective-permute-done), kind=kOutput, calls=%fused_computation.7 | convolution fusion | flops 1359839232 | bytes 10027008 | tf_op jit(solution)/shard_map/dot_general | solution.py:28
  62.2 2.9 %fusion.3 = bf16[768,1152]{1,0:T(8,128)(2,1)} fusion(f32[768,1152]{1,0:T(8,128)S(1)} %convolution_add_fusion.1, bf16[768,768]{1,0:T(8,128)(2,1)S(1)} %divide_convert_fusion, bf16[768,1152]{1,0:T(8,128)(2,1)S(1)} %collective-permute-done.1, f32[]{:T(128)} %bitcast.20), kind=kOutput, calls=%fused_computation.8 | convolution fusion | flops 1361608704 | bytes 8257540 | tf_op jit(solution)/shard_map/dot_general | solution.py:28
  65.1 60.3 %collective-permute-done.3 = f32[768,1152]{1,0:T(8,128)S(1)} collective-permute-done((f32[768,1152]{1,0:T(8,128)S(1)}, f32[768,1152]{1,0:T(8,128)S(1)}, u32[]{:S(2)}, u32[]{:S(2)}) %collective-permute-start.3) | collective-permute-done | bytes 3538976 | tf_op jit(solution)/shard_map/ppermute | solution.py:14
  125.5 6.7 %collective-permute-done.2 = f32[768,1152]{1,0:T(8,128)S(1)} collective-permute-done((f32[768,1152]{1,0:T(8,128)S(1)}, f32[768,1152]{1,0:T(8,128)S(1)}, u32[]{:S(2)}, u32[]{:S(2)}) %collective-permute-start.2) | collective-permute-done | bytes 3538976 | tf_op jit(solution)/shard_map/ppermute | solution.py:14
  132.2 3.0 %fusion.4 = bf16[768,1152]{1,0:T(8,128)(2,1)} fusion(f32[768,1152]{1,0:T(8,128)S(1)} %collective-permute-done.3, f32[768,1152]{1,0:T(8,128)S(1)} %collective-permute-done.2, bf16[768,768]{1,0:T(8,128)(2,1)S(1)} %subtract_convert_fusion, bf16[768,1152]{1,0:T(8,128)(2,1)S(1)} %copy-done, f32[]{:T(128)} %bitcast.22), kind=kOutput, calls=%fused_computation.9 | convolution fusion | flops 1362493440 | bytes 11796484 | tf_op jit(solution)/shard_map/dot_general | solution.py:32
Async XLA Ops:
  0.6 42.2 %copy-start = (bf16[768,1152]{1,0:T(8,128)(2,1)S(1)}, bf16[768,1152]{1,0:T(8,128)(2,1)}, u32[]{:S(2)}) copy-start(bf16[768,1152]{1,0:T(8,128)(2,1)} %param.4) | copy-start | bytes 5308420
  0.6 42.1 %collective-permute-start.1 = (bf16[768,1152]{1,0:T(8,128)(2,1)}, bf16[768,1152]{1,0:T(8,128)(2,1)S(1)}, u32[]{:S(2)}, u32[]{:S(2)}) collective-permute-start(bf16[768,1152]{1,0:T(8,128)(2,1)} %param.5), channel_id=1, source_target_pairs={{0,8},{8,0},{1,9},{9,1},{2,10},{10,2},{3,11},{11,3},{4,12},{12,4},... | collective-permute-start | bytes 5308424 | tf_op jit(solution)/shard_map/ppermute | solution.py:14
  3.8 45.9 %collective-permute-start = (bf16[768,1152]{1,0:T(8,128)(2,1)}, bf16[768,1152]{1,0:T(8,128)(2,1)S(1)}, u32[]{:S(2)}, u32[]{:S(2)}) collective-permute-start(bf16[768,1152]{1,0:T(8,128)(2,1)} %param.5), channel_id=1, source_target_pairs={{0,128},{128,0},{1,129},{129,1},{2,130},{130,2},{3,131},{131,3},{4... | collective-permute-start | bytes 5308424 | tf_op jit(solution)/shard_map/ppermute | solution.py:14
  46.5 79.0 %collective-permute-start.3 = (f32[768,1152]{1,0:T(8,128)S(1)}, f32[768,1152]{1,0:T(8,128)S(1)}, u32[]{:S(2)}, u32[]{:S(2)}) collective-permute-start(f32[768,1152]{1,0:T(8,128)S(1)} %convolution_multiply_fusion), channel_id=1, source_target_pairs={{0,8},{8,0},{1,9},{9,1},{2,10},{10,2},{3,11},{11,3},{4,12},{12,4},... | collective-permute-start | bytes 10616840 | tf_op jit(solution)/shard_map/ppermute | solution.py:14
  51.6 5.2 %copy-start.1 = (bf16[768,1152]{1,0:T(8,128)(2,1)S(1)}, bf16[768,1152]{1,0:T(8,128)(2,1)}, u32[]{:S(2)}) copy-start(bf16[768,1152]{1,0:T(8,128)(2,1)} %param.5) | copy-start | bytes 5308420
  53.3 78.9 %collective-permute-start.2 = (f32[768,1152]{1,0:T(8,128)S(1)}, f32[768,1152]{1,0:T(8,128)S(1)}, u32[]{:S(2)}, u32[]{:S(2)}) collective-permute-start(f32[768,1152]{1,0:T(8,128)S(1)} %convolution_multiply_fusion.1), channel_id=1, source_target_pairs={{0,128},{128,0},{1,129},{129,1},{2,130},{130,2},{3,131},{131,3},{4... | collective-permute-start | bytes 10616840 | tf_op jit(solution)/shard_map/ppermute | solution.py:14
where the time goes:
time: 135 us
  waiting for transfers between devices  102 us (76%)
  matrix products  18.7 us (14%)
  starting transfers between devices  12.9 us (10%)
  between operations  1.99 us (1%)
    ppermute x4, waiting for transfers between devices, partner(): return lax.ppermute(block, axis, route)  102 us
    ppermute x4, starting transfers between devices, partner(): return lax.ppermute(block, axis, route)  12.9 us
    dot_general x3, matrix products, text_term(): lax.dot_general(grad, left, (((0,), (0,)), ((), ())), preferred_element_t...  6.47 us
    dot_general x3, matrix products, image_term(): return scale * jnp.dot(grad, right, preferred_element_type=jnp.float32)  6.4 us
    dot_general x3, matrix products, block_grad(): lax.dot_general(left, right, (((1,), (1,)), ((), ())), preferred_element_...  5.82 us
  transfers between devices with their start and end apart: 4, of which 3 were waited for; matrix products, arithmetic and copies ran while one was open for 12% of the time, Pallas kernels for 0%

commit v1 on v0

v1 whole, which is shorter than its diff:
```python
import functools

import jax
import jax.numpy as jnp
from jax import lax
from jax.experimental import pallas as pl
from jax.experimental.pallas import tpu as pltpu
from jax.sharding import PartitionSpec as P

MESH = pl.DeviceIdType.MESH
CHUNK = 128
TAIL = (64, 32, 32)
AHEAD = 3
TILE = 256


def products(left, block, scale, bias, accumulate, diagonal=None):
    height, width = left.shape[0], block.shape[0]

    def tile(index, _):
        rows = pl.ds(pl.multiple_of(index * TILE, TILE), TILE)
        logits = lax.dot_general(
            left[rows, :], block[...], (((1,), (1,)), ((), ())), preferred_element_type=jnp.float32
        )
        value = jax.nn.sigmoid(logits * scale + bias)
        if diagonal is not None:
            here = lax.broadcasted_iota(jnp.int32, (TILE, width), 0) + index * TILE
            there = lax.broadcasted_iota(jnp.int32, (TILE, width), 1) + diagonal
            value = value - jnp.where(here == there, 1.0, 0.0)
        accumulate(rows, value.astype(jnp.bfloat16))
        return 0

    lax.fori_loop(0, height // TILE, tile, 0)


def exchange_kernel(
    images, texts, scale_ref, bias_ref, acc, image_out, last_grad, last_block, scale_out,
    own, got, send_sem, recv_sem, load_sem,
):
    rows = images.shape[0]
    row, col = lax.axis_index("row"), lax.axis_index("col")
    n_row, n_col = lax.axis_size("row"), lax.axis_size("col")
    partners = (
        (row, lax.rem(col + n_col // 2, n_col)),
        (lax.rem(row + n_row // 2, n_row), col),
    )
    per_unit = rows // CHUNK
    whole = 2 * per_unit - sum(TAIL) // CHUNK
    tail_at = [rows - sum(TAIL[j:]) for j in range(len(TAIL))]
    sources = (texts, images)

    barrier = pltpu.get_barrier_semaphore()
    for partner in partners:
        pl.semaphore_signal(barrier, inc=1, device_id=partner, device_id_type=MESH)
    pl.semaphore_wait(barrier, len(partners))

    def copies(unit, start, size, step):
        found = []
        for axis, partner in enumerate(partners):
            place = 2 * start + axis * size
            if not isinstance(place, int):
                place = pl.multiple_of(place, CHUNK)
            target = (
                last_block.at[pl.ds(axis * size, size)]
                if isinstance(step, int) and step == whole + len(TAIL) - 1
                else got.at[unit, pl.ds(place, size)]
            )
            found.append(
                pltpu.make_async_remote_copy(
                    src_ref=sources[unit].at[pl.ds(start, size)],
                    dst_ref=target,
                    send_sem=send_sem.at[axis, step],
                    recv_sem=recv_sem.at[axis, step],
                    device_id=partner,
                    device_id_type=MESH,
                )
            )
        return found

    def tail_copies(j):
        return copies(1, tail_at[j], TAIL[j], whole + j)

    def start_step(step):
        if isinstance(step, int):
            if step < whole:
                found = copies(step // per_unit, step % per_unit * CHUNK, CHUNK, step)
            else:
                found = tail_copies(step - whole)
            for copy in found:
                copy.start()
            return
        for unit in range(2):
            low, high = unit * per_unit, min((unit + 1) * per_unit, whole)

            @pl.when((step >= low) & (step < high))
            def _():
                start = pl.multiple_of((step - low) * CHUNK, CHUNK)
                for copy in copies(unit, start, CHUNK, step):
                    copy.start()

        for j in range(len(TAIL)):

            @pl.when(step == whole + j)
            def _():
                start_step(whole + j)

    for step in range(AHEAD):
        start_step(step)

    loads = [
        pltpu.make_async_copy(images, own.at[0], load_sem.at[0]),
        pltpu.make_async_copy(texts, own.at[1], load_sem.at[1]),
    ]
    for load in loads:
        load.start()
    for load in loads:
        load.wait()
    scale, bias = scale_ref[0], bias_ref[0]
    scale_out[...] = jnp.full(scale_out.shape, scale, jnp.float32)

    def add_to(unit, block):
        def accumulate(tile_rows, grad):
            acc[unit, tile_rows, :] += jnp.dot(
                grad, block[...], preferred_element_type=jnp.float32
            )

        return accumulate

    for unit in range(2):
        acc[unit] = jnp.zeros((rows, acc.shape[2]), jnp.float32)

        def own_block(index, _):
            at = pl.multiple_of(index * TILE, TILE)
            block = own.at[1 - unit, pl.ds(at, TILE)]
            products(own.at[unit], block, scale, bias, add_to(unit, block), diagonal=at)
            return 0

        lax.fori_loop(0, rows // TILE, own_block, 0)

    def wait_step(unit, start, size, step):
        for copy in copies(unit, start, size, step):
            copy.wait()

    for unit in range(2):
        low, high = unit * per_unit, min((unit + 1) * per_unit, whole)

        def met_block(step, _):
            start = pl.multiple_of((step - low) * CHUNK, CHUNK)
            wait_step(unit, start, CHUNK, step)
            start_step(step + AHEAD)
            block = got.at[unit, pl.ds(pl.multiple_of(2 * start, 2 * CHUNK), 2 * CHUNK)]
            products(own.at[unit], block, scale, bias, add_to(unit, block))
            return 0

        lax.fori_loop(low, high, met_block, 0)
        if unit == 0:
            image_out[...] = (acc[0] * scale).astype(jnp.bfloat16)

    for j in range(len(TAIL)):
        wait_step(1, tail_at[j], TAIL[j], whole + j)
        if whole + j + AHEAD < whole + len(TAIL):
            start_step(whole + j + AHEAD)
        if j < len(TAIL) - 1:
            block = got.at[1, pl.ds(2 * tail_at[j], 2 * TAIL[j])]
            products(own.at[1], block, scale, bias, add_to(1, block))
        else:

            def keep(tile_rows, grad):
                last_grad[tile_rows, :] = grad

            products(own.at[1], last_block, scale, bias, keep)


def finish_kernel(acc, image_in, last_grad, last_block, scale_in, image_out, text_out, text, sem):
    rows = text.shape[0]
    image_copy = pltpu.make_async_copy(image_in, image_out, sem.at[0])
    image_copy.start()
    scale = scale_in[0:1, 0:1]
    text_copies = []
    for index in range(rows // TILE):
        tile_rows = pl.ds(index * TILE, TILE)
        total = acc[1, tile_rows, :] + jnp.dot(
            last_grad[tile_rows, :], last_block[...], preferred_element_type=jnp.float32
        )
        text[tile_rows, :] = (total * scale).astype(jnp.bfloat16)
        copy = pltpu.make_async_copy(
            text.at[tile_rows], text_out.at[tile_rows], sem.at[1 + index]
        )
        copy.start()
        text_copies.append(copy)
    image_copy.wait()
    for copy in text_copies:
        copy.wait()


def shards(images, texts, logit_scale, logit_bias):
    rows, width = images.shape
    steps = 2 * (rows // CHUNK) - sum(TAIL) // CHUNK + len(TAIL)
    hbm = pl.BlockSpec(memory_space=pltpu.HBM)
    vmem = pl.BlockSpec(memory_space=pltpu.VMEM)
    smem = pl.BlockSpec(memory_space=pltpu.SMEM)
    kept = pl.pallas_call(
        exchange_kernel,
        out_shape=[
            pltpu.VMEM((2, rows, width), jnp.float32),
            pltpu.VMEM((rows, width), jnp.bfloat16),
            pltpu.VMEM((rows, 2 * TAIL[-1]), jnp.bfloat16),
            pltpu.VMEM((2 * TAIL[-1], width), jnp.bfloat16),
            pltpu.VMEM((8, 128), jnp.float32),
        ],
        in_specs=[hbm, hbm, smem, smem],
        out_specs=[vmem] * 5,
        scratch_shapes=[
            pltpu.VMEM((2, rows, width), jnp.bfloat16),
            pltpu.VMEM((2, 2 * rows, width), jnp.bfloat16),
            pltpu.SemaphoreType.DMA((2, steps)),
            pltpu.SemaphoreType.DMA((2, steps)),
            pltpu.SemaphoreType.DMA((2,)),
        ],
        compiler_params=pltpu.CompilerParams(
            collective_id=0, has_side_effects=True, vmem_limit_bytes=32 << 20
        ),
        name="exchange",
    )(
        pltpu.with_memory_space_constraint(images, pltpu.HBM),
        pltpu.with_memory_space_constraint(texts, pltpu.HBM),
        logit_scale,
        logit_bias,
    )
    kept = [pltpu.with_memory_space_constraint(x, pltpu.VMEM) for x in kept]
    return pl.pallas_call(
        finish_kernel,
        out_shape=[jax.ShapeDtypeStruct((rows, width), jnp.bfloat16)] * 2,
        in_specs=[vmem] * 5,
        out_specs=[hbm] * 2,
        scratch_shapes=[
            pltpu.VMEM((rows, width), jnp.bfloat16),
            pltpu.SemaphoreType.DMA((1 + rows // TILE,)),
        ],
        compiler_params=pltpu.CompilerParams(vmem_limit_bytes=16 << 20),
        name="finish",
    )(*kept)


def solution(mesh):
    placed = (P(("row", "col"), None), P(("row", "col"), None), P(), P())
    return jax.shard_map(
        shards,
        mesh=mesh,
        in_specs=placed,
        out_specs=(P(("row", "col"), None), P(("row", "col"), None)),
        check_vma=False,
    )
```

time: 135 us -> 90.9 us (0.67)
  waiting for transfers between devices: 102 us -> 0 us
  Pallas kernels: 0 us -> 88.8 us
  matrix products: 18.7 us -> 0 us
  starting transfers between devices: 12.9 us -> 0 us
    ppermute x4 -> x0, waiting for transfers between devices: 102 us -> none  [partner(): return lax.ppermute(block, axis, route)]
    pallas_call x0 -> x2, Pallas kernels: none -> 88.8 us  [the longest x1 87 us: shards(): pl.pallas_call(exchange_kernel, out_shape=[pltpu.VMEM((2, rows, width), j...]
    dot_general x9 -> x0, matrix products: 18.7 us -> none  [the longest x3 6.47 us: text_term(): lax.dot_general(grad, left, (((0,), (0,)), ((), ())), preferred_element_t...]
    ppermute x4 -> x0, starting transfers between devices: 12.9 us -> none  [partner(): return lax.ppermute(block, axis, route)]
  transfers between devices with their start and end apart: 4 -> 0, of which waited for: 3 -> 0; matrix products, arithmetic and copies ran while one was open for 12% -> 0% of each run, Pallas kernels for 0% -> 0%
where the time goes in v1:
time: 90.9 us; the launch traced here: 90.8 us
  Pallas kernels  88.8 us (98%)
  between operations  1.93 us (2%)
    pallas_call x1, Pallas kernels, shards(): pl.pallas_call(exchange_kernel, out_shape=[pltpu.VMEM((2, rows, width), j...  87 us
    pallas_call x1, Pallas kernels, shards(): pl.pallas_call(finish_kernel, out_shape=[jax.ShapeDtypeStruct((rows, widt...  1.82 us

profile of v1, /device:TPU:160, one launch (start us, length us, event | category | flops | bytes accessed | tf_op | source)
XLA Modules:
  0.0 90.8 jit_solution(9420032434036494946)
XLA Ops:
  1.9 87.0 %exchange.1 = (f32[2,768,1152]{2,1,0:T(8,128)S(1)}, bf16[768,1152]{1,0:T(8,128)(2,1)S(1)}, bf16[768,64]{1,0:T(8,128)(2,1)S(1)}, bf16[64,1152]{1,0:T(8,128)(2,1)S(1)}, f32[8,128]{1,0:T(8,128)S(1)}) custom-call(bf16[768,1152]{1,0:T(8,128)(2,1)} %images.1, bf16[768,1152]{1,0:T(8,128)(2,1)} %texts.1, f32[1]{0:T(128)S(6)} %copy.6.scale_ref, f32[1]{0:T(128)S(6)} %copy.7.bias_ref), custom_call_target="tpu_custom_call" | custom-call | tf_op jit(solution)/shard_map/exchange/pallas_call | solution.py:202
  88.9 1.8 %finish.1 = (bf16[768,1152]{1,0:T(8,128)(2,1)}, bf16[768,1152]{1,0:T(8,128)(2,1)}) custom-call(f32[2,768,1152]{2,1,0:T(8,128)S(1)} %get-tuple-element.7.acc, bf16[768,1152]{1,0:T(8,128)(2,1)S(1)} %get-tuple-element.8.image_in, bf16[768,64]{1,0:T(8,128)(2,1)S(1)} %get-tuple-element.9.last_grad, bf16[64,1152]{1,0:T(8,128)(2,1)S(1)} %get-tuple-element.10.last_block, ...), custom_call_target="tpu_custom_call" | custom-call | tf_op jit(solution)/shard_map/finish/pallas_call | solution.py:231

commit v2 on v0

v2 whole, which is shorter than its diff:
```python
import jax
import jax.numpy as jnp
from jax import lax
from jax.experimental import pallas as pl
from jax.experimental.pallas import tpu as pltpu
from jax.sharding import PartitionSpec as P

MESH = pl.DeviceIdType.MESH
CHUNK = 128
FIRST = 2
BLOCK = 2 * CHUNK


def gradient(left, block, scale, bias, diagonal=None):
    logits = lax.dot_general(
        left[...], block[...], (((1,), (1,)), ((), ())), preferred_element_type=jnp.float32
    )
    value = jax.nn.sigmoid(logits * scale + bias)
    if diagonal is not None:
        here = lax.broadcasted_iota(jnp.int32, value.shape, 0)
        there = lax.broadcasted_iota(jnp.int32, value.shape, 1) + diagonal
        value = value - jnp.where(here == there, 1.0, 0.0)
    return value.astype(jnp.bfloat16)


def exchange_kernel(
    images, texts, scale_ref, bias_ref, acc, image_out, last_grad, got, scale_out,
    own, send_sem, recv_sem, load_sem, ready,
):
    rows = images.shape[0]
    row, col = lax.axis_index("row"), lax.axis_index("col")
    n_row, n_col = lax.axis_size("row"), lax.axis_size("col")
    partners = (
        (row, lax.rem(col + n_col // 2, n_col)),
        (lax.rem(row + n_row // 2, n_row), col),
    )
    per_unit = rows // CHUNK
    steps = 2 * per_unit
    sources = (texts, images)

    def transfer(axis, unit, index):
        step = unit * per_unit + index
        start = index * CHUNK
        if not isinstance(start, int):
            start = pl.multiple_of(start, CHUNK)
        return pltpu.make_async_remote_copy(
            src_ref=sources[unit].at[pl.ds(start, CHUNK)],
            dst_ref=got.at[step, pl.ds(axis * CHUNK, CHUNK)],
            send_sem=send_sem.at[axis, step],
            recv_sem=recv_sem.at[axis, step],
            device_id=partners[axis],
            device_id_type=MESH,
        )

    halves = (col >= n_col // 2, row >= n_row // 2)
    barrier = pltpu.get_barrier_semaphore()
    for axis in range(2):

        @pl.when(jnp.logical_not(halves[axis]))
        def _():
            pl.semaphore_signal(barrier, inc=1, device_id=partners[axis], device_id_type=MESH)

    @pl.when(jnp.logical_or(halves[0], halves[1]))
    def _():
        pl.semaphore_wait(barrier, halves[0].astype(jnp.int32) + halves[1].astype(jnp.int32))

    for axis in range(2):

        @pl.when(halves[axis])
        def _():
            pl.semaphore_signal(
                ready.at[axis], inc=1, device_id=partners[axis], device_id_type=MESH
            )
            for step in range(FIRST):
                transfer(axis, step // per_unit, step % per_unit).start()

    for axis in range(2):

        @pl.when(jnp.logical_not(halves[axis]))
        def _():
            pl.semaphore_wait(ready.at[axis], 1)
            for step in range(FIRST):
                transfer(axis, step // per_unit, step % per_unit).start()

    for step in range(FIRST, steps):
        for axis in range(2):
            transfer(axis, step // per_unit, step % per_unit).start()

    loads = [
        pltpu.make_async_copy(images, own.at[0], load_sem.at[0]),
        pltpu.make_async_copy(texts, own.at[1], load_sem.at[1]),
    ]
    for load in loads:
        load.start()
    for load in loads:
        load.wait()
    scale, bias = scale_ref[0], bias_ref[0]
    scale_out[...] = jnp.full(scale_out.shape, scale, jnp.float32)

    for unit in range(2):

        def own_block(index, _):
            at = pl.multiple_of(index * BLOCK, BLOCK)
            block = own.at[1 - unit, pl.ds(at, BLOCK)]
            grad = gradient(own.at[unit], block, scale, bias, at)
            acc[unit] += jnp.dot(grad, block[...], preferred_element_type=jnp.float32)
            return 0

        acc[unit] = jnp.zeros(acc.shape[1:], jnp.float32)
        lax.fori_loop(0, rows // BLOCK, own_block, 0)

    for unit in range(2):

        def met_block(index, _):
            step = unit * per_unit + index
            for axis in range(2):
                transfer(axis, unit, index).wait()
            block = got.at[step]
            grad = gradient(own.at[unit], block, scale, bias)
            if unit == 0:
                acc[unit] += jnp.dot(grad, block[...], preferred_element_type=jnp.float32)
            else:
                last_grad[...] = grad

                @pl.when(step < steps - 1)
                def _():
                    acc[unit] += jnp.dot(grad, block[...], preferred_element_type=jnp.float32)

            return 0

        lax.fori_loop(0, per_unit, met_block, 0)
        if unit == 0:
            image_out[...] = (acc[0] * scale).astype(jnp.bfloat16)


def finish_kernel(acc, image_in, last_grad, got, scale_in, image_out, text_out, text, sem):
    rows = text.shape[0]
    image_copy = pltpu.make_async_copy(image_in, image_out, sem.at[0])
    image_copy.start()
    scale = scale_in[0:1, 0:1]
    last = got.shape[0] - 1
    text_copies = []
    for index in range(rows // BLOCK):
        part = pl.ds(index * BLOCK, BLOCK)
        total = acc[1, part, :] + jnp.dot(
            last_grad[part, :], got[last], preferred_element_type=jnp.float32
        )
        text[part, :] = (total * scale).astype(jnp.bfloat16)
        copy = pltpu.make_async_copy(text.at[part], text_out.at[part], sem.at[1 + index])
        copy.start()
        text_copies.append(copy)
    image_copy.wait()
    for copy in text_copies:
        copy.wait()


def shards(images, texts, logit_scale, logit_bias):
    rows, width = images.shape
    steps = 2 * (rows // CHUNK)
    hbm = pl.BlockSpec(memory_space=pltpu.HBM)
    vmem = pl.BlockSpec(memory_space=pltpu.VMEM)
    smem = pl.BlockSpec(memory_space=pltpu.SMEM)
    kept = pl.pallas_call(
        exchange_kernel,
        out_shape=[
            pltpu.VMEM((2, rows, width), jnp.float32),
            pltpu.VMEM((rows, width), jnp.bfloat16),
            pltpu.VMEM((rows, BLOCK), jnp.bfloat16),
            pltpu.VMEM((steps, BLOCK, width), jnp.bfloat16),
            pltpu.VMEM((8, 128), jnp.float32),
        ],
        in_specs=[hbm, hbm, smem, smem],
        out_specs=[vmem] * 5,
        scratch_shapes=[
            pltpu.VMEM((2, rows, width), jnp.bfloat16),
            pltpu.SemaphoreType.DMA((2, steps)),
            pltpu.SemaphoreType.DMA((2, steps)),
            pltpu.SemaphoreType.DMA((2,)),
            pltpu.SemaphoreType.REGULAR((2,)),
        ],
        compiler_params=pltpu.CompilerParams(
            collective_id=0, has_side_effects=True, vmem_limit_bytes=32 << 20
        ),
        name="exchange",
    )(
        pltpu.with_memory_space_constraint(images, pltpu.HBM),
        pltpu.with_memory_space_constraint(texts, pltpu.HBM),
        logit_scale,
        logit_bias,
    )
    kept = [pltpu.with_memory_space_constraint(x, pltpu.VMEM) for x in kept]
    return pl.pallas_call(
        finish_kernel,
        out_shape=[jax.ShapeDtypeStruct((rows, width), jnp.bfloat16)] * 2,
        in_specs=[vmem] * 5,
        out_specs=[hbm] * 2,
        scratch_shapes=[
            pltpu.VMEM((rows, width), jnp.bfloat16),
            pltpu.SemaphoreType.DMA((1 + rows // BLOCK,)),
        ],
        compiler_params=pltpu.CompilerParams(vmem_limit_bytes=16 << 20),
        name="finish",
    )(*kept)


def solution(mesh):
    placed = (P(("row", "col"), None), P(("row", "col"), None), P(), P())
    return jax.shard_map(
        shards,
        mesh=mesh,
        in_specs=placed,
        out_specs=(P(("row", "col"), None), P(("row", "col"), None)),
        check_vma=False,
    )
```

time: 135 us -> 86.3 us (0.64); the launches traced: 135 us -> 85.1 us
  waiting for transfers between devices: 102 us -> 0 us
  Pallas kernels: 0 us -> 83.2 us
  matrix products: 18.7 us -> 0 us
  starting transfers between devices: 12.9 us -> 0 us
    ppermute x4 -> x0, waiting for transfers between devices: 102 us -> none  [partner(): return lax.ppermute(block, axis, route)]
    pallas_call x0 -> x2, Pallas kernels: none -> 83.2 us  [the longest x1 81.3 us: shards(): pl.pallas_call(exchange_kernel, out_shape=[pltpu.VMEM((2, rows, width), j...]
    dot_general x9 -> x0, matrix products: 18.7 us -> none  [the longest x3 6.47 us: text_term(): lax.dot_general(grad, left, (((0,), (0,)), ((), ())), preferred_element_t...]
    ppermute x4 -> x0, starting transfers between devices: 12.9 us -> none  [partner(): return lax.ppermute(block, axis, route)]
  transfers between devices with their start and end apart: 4 -> 0, of which waited for: 3 -> 0; matrix products, arithmetic and copies ran while one was open for 12% -> 0% of each run, Pallas kernels for 0% -> 0%
where the time goes in v2:
time: 86.3 us; the launch traced here: 85.1 us
  Pallas kernels  83.2 us (96%)
  between operations  1.93 us (2%)
    pallas_call x1, Pallas kernels, shards(): pl.pallas_call(exchange_kernel, out_shape=[pltpu.VMEM((2, rows, width), j...  81.3 us
    pallas_call x1, Pallas kernels, shards(): pl.pallas_call(finish_kernel, out_shape=[jax.ShapeDtypeStruct((rows, widt...  1.83 us

profile of v2, /device:TPU:160, one launch (start us, length us, event | category | flops | bytes accessed | tf_op | source)
XLA Modules:
  0.0 85.1 jit_solution(10668361971085189400)
XLA Ops:
  1.9 81.3 %exchange.1 = (f32[2,768,1152]{2,1,0:T(8,128)S(1)}, bf16[768,1152]{1,0:T(8,128)(2,1)S(1)}, bf16[768,256]{1,0:T(8,128)(2,1)S(1)}, bf16[12,256,1152]{2,1,0:T(8,128)(2,1)S(1)}, f32[8,128]{1,0:T(8,128)S(1)}) custom-call(bf16[768,1152]{1,0:T(8,128)(2,1)} %images.1, bf16[768,1152]{1,0:T(8,128)(2,1)} %texts.1, f32[1]{0:T(128)S(6)} %copy.6.scale_ref, f32[1]{0:T(128)S(6)} %copy.7.bias_ref), custom_call_target="tpu_custom_call" | custom-call | tf_op jit(solution)/shard_map/exchange/pallas_call | solution.py:163
  83.3 1.8 %finish.1 = (bf16[768,1152]{1,0:T(8,128)(2,1)}, bf16[768,1152]{1,0:T(8,128)(2,1)}) custom-call(f32[2,768,1152]{2,1,0:T(8,128)S(1)} %get-tuple-element.7.acc, bf16[768,1152]{1,0:T(8,128)(2,1)S(1)} %get-tuple-element.8.image_in, bf16[768,256]{1,0:T(8,128)(2,1)S(1)} %get-tuple-element.9.last_grad, bf16[12,256,1152]{2,1,0:T(8,128)(2,1)S(1)} %get-tuple-element.10.got, ...), custom_call_target="tpu_custom_call" | custom-call | tf_op jit(solution)/shard_map/finish/pallas_call | solution.py:192

commit v3 on v2

--- a/solution.py
+++ b/solution.py
@@ -6,9 +6,9 @@
 from jax.sharding import PartitionSpec as P
 
 MESH = pl.DeviceIdType.MESH
-CHUNK = 128
-FIRST = 2
-BLOCK = 2 * CHUNK
+CHUNKS = ((384, 384), (384, 256, 128))
+BLOCK = 256
+LAST = 1024
 
 
 def gradient(left, block, scale, bias, diagonal=None):
@@ -25,7 +25,7 @@
 
 def exchange_kernel(
     images, texts, scale_ref, bias_ref, acc, image_out, last_grad, got, scale_out,
-    own, send_sem, recv_sem, load_sem, ready,
+    own, logits, send_sem, recv_sem, load_sem, ready,
 ):
     rows = images.shape[0]
     row, col = lax.axis_index("row"), lax.axis_index("col")
@@ -34,20 +34,26 @@
         (row, lax.rem(col + n_col // 2, n_col)),
         (lax.rem(row + n_row // 2, n_row), col),
     )
-    per_unit = rows // CHUNK
-    steps = 2 * per_unit
+    per_unit = 2 * rows // BLOCK
+    plan = []
+    for unit, sizes in enumerate(CHUNKS):
+        start = 0
+        for size in sizes:
+            plan.append((unit, start, size, 0, images.shape[1]))
+            start += size
+    unit, start, size, _, width = plan.pop()
+    plan += [(unit, start, size, 0, LAST), (unit, start, size, LAST, width - LAST)]
     sources = (texts, images)
 
-    def transfer(axis, unit, index):
-        step = unit * per_unit + index
-        start = index * CHUNK
-        if not isinstance(start, int):
-            start = pl.multiple_of(start, CHUNK)
+    def transfer(axis, number):
+        unit, start, size, left, width = plan[number]
+        columns = pl.ds(left, width)
+        place = 2 * (unit * rows + start) + axis * size
         return pltpu.make_async_remote_copy(
-            src_ref=sources[unit].at[pl.ds(start, CHUNK)],
-            dst_ref=got.at[step, pl.ds(axis * CHUNK, CHUNK)],
-            send_sem=send_sem.at[axis, step],
-            recv_sem=recv_sem.at[axis, step],
+            src_ref=sources[unit].at[pl.ds(start, size), columns],
+            dst_ref=got.at[pl.ds(place, size), columns],
+            send_sem=send_sem.at[axis, number],
+            recv_sem=recv_sem.at[axis, number],
             device_id=partners[axis],
             device_id_type=MESH,
         )
@@ -71,20 +77,18 @@
             pl.semaphore_signal(
                 ready.at[axis], inc=1, device_id=partners[axis], device_id_type=MESH
             )
-            for step in range(FIRST):
-                transfer(axis, step // per_unit, step % per_unit).start()
+            transfer(axis, 0).start()
 
     for axis in range(2):
 
         @pl.when(jnp.logical_not(halves[axis]))
         def _():
             pl.semaphore_wait(ready.at[axis], 1)
-            for step in range(FIRST):
-                transfer(axis, step // per_unit, step % per_unit).start()
-
-    for step in range(FIRST, steps):
+            transfer(axis, 0).start()
+
+    for number in range(1, len(plan)):
         for axis in range(2):
-            transfer(axis, step // per_unit, step % per_unit).start()
+            transfer(axis, number).start()
 
     loads = [
         pltpu.make_async_copy(images, own.at[0], load_sem.at[0]),
@@ -110,27 +114,40 @@
         lax.fori_loop(0, rows // BLOCK, own_block, 0)
 
     for unit in range(2):
+        blocks = per_unit - unit
 
         def met_block(index, _):
-            step = unit * per_unit + index
-            for axis in range(2):
-                transfer(axis, unit, index).wait()
-            block = got.at[step]
+            for number, (owner, start, *_rest) in enumerate(plan[:-2]):
+                if owner == unit:
+
+                    @pl.when(index == 2 * start // BLOCK)
+                    def _():
+                        for axis in range(2):
+                            transfer(axis, number).wait()
+
+            at = pl.multiple_of((unit * per_unit + index) * BLOCK, BLOCK)
+            block = got.at[pl.ds(at, BLOCK)]
             grad = gradient(own.at[unit], block, scale, bias)
-            if unit == 0:
-                acc[unit] += jnp.dot(grad, block[...], preferred_element_type=jnp.float32)
-            else:
-                last_grad[...] = grad
-
-                @pl.when(step < steps - 1)
-                def _():
-                    acc[unit] += jnp.dot(grad, block[...], preferred_element_type=jnp.float32)
-
+            acc[unit] += jnp.dot(grad, block[...], preferred_element_type=jnp.float32)
             return 0
 
-        lax.fori_loop(0, per_unit, met_block, 0)
+        lax.fori_loop(0, blocks, met_block, 0)
         if unit == 0:
             image_out[...] = (acc[0] * scale).astype(jnp.bfloat16)
+
+    last = pl.ds(got.shape[0] - BLOCK, BLOCK)
+    for number, columns in ((-2, pl.ds(0, LAST)), (-1, pl.ds(LAST, images.shape[1] - LAST))):
+        for axis in range(2):
+            transfer(axis, len(plan) + number).wait()
+        part = lax.dot_general(
+            own[1, :, columns], got[last, columns], (((1,), (1,)), ((), ())),
+            preferred_element_type=jnp.float32,
+        )
+        if number == -2:
+            logits[...] = part
+        else:
+            value = jax.nn.sigmoid((logits[...] + part) * scale + bias)
+            last_grad[...] = value.astype(jnp.bfloat16)
 
 
 def finish_kernel(acc, image_in, last_grad, got, scale_in, image_out, text_out, text, sem):
@@ -138,12 +155,12 @@
     image_copy = pltpu.make_async_copy(image_in, image_out, sem.at[0])
     image_copy.start()
     scale = scale_in[0:1, 0:1]
-    last = got.shape[0] - 1
+    last = got.shape[0] - BLOCK
     text_copies = []
     for index in range(rows // BLOCK):
         part = pl.ds(index * BLOCK, BLOCK)
         total = acc[1, part, :] + jnp.dot(
-            last_grad[part, :], got[last], preferred_element_type=jnp.float32
+            last_grad[part, :], got[pl.ds(last, BLOCK)], preferred_element_type=jnp.float32
         )
         text[part, :] = (total * scale).astype(jnp.bfloat16)
         copy = pltpu.make_async_copy(text.at[part], text_out.at[part], sem.at[1 + index])
@@ -156,7 +173,7 @@
 
 def shards(images, texts, logit_scale, logit_bias):
     rows, width = images.shape
-    steps = 2 * (rows // CHUNK)
+    chunks = sum(len(sizes) for sizes in CHUNKS) + 1
     hbm = pl.BlockSpec(memory_space=pltpu.HBM)
     vmem = pl.BlockSpec(memory_space=pltpu.VMEM)
     smem = pl.BlockSpec(memory_space=pltpu.SMEM)
@@ -166,15 +183,16 @@
             pltpu.VMEM((2, rows, width), jnp.float32),
             pltpu.VMEM((rows, width), jnp.bfloat16),
             pltpu.VMEM((rows, BLOCK), jnp.bfloat16),
-            pltpu.VMEM((steps, BLOCK, width), jnp.bfloat16),
+            pltpu.VMEM((4 * rows, width), jnp.bfloat16),
             pltpu.VMEM((8, 128), jnp.float32),
         ],
         in_specs=[hbm, hbm, smem, smem],
         out_specs=[vmem] * 5,
         scratch_shapes=[
             pltpu.VMEM((2, rows, width), jnp.bfloat16),
-            pltpu.SemaphoreType.DMA((2, steps)),
-            pltpu.SemaphoreType.DMA((2, steps)),
+            pltpu.VMEM((rows, BLOCK), jnp.float32),
+            pltpu.SemaphoreType.DMA((2, chunks)),
+            pltpu.SemaphoreType.DMA((2, chunks)),
             pltpu.SemaphoreType.DMA((2,)),
             pltpu.SemaphoreType.REGULAR((2,)),
         ],

time: 86.3 us -> 86.5 us (level)
  no operation moved by 1% of the time
where the time goes in v3:
time: 86.5 us; the launch traced here: 84.9 us
  Pallas kernels  82.9 us (96%)
  between operations  1.93 us (2%)
    pallas_call x1, Pallas kernels, shards(): pl.pallas_call(exchange_kernel, out_shape=[pltpu.VMEM((2, rows, width), j...  81.1 us
    pallas_call x1, Pallas kernels, shards(): pl.pallas_call(finish_kernel, out_shape=[jax.ShapeDtypeStruct((rows, widt...  1.83 us

profile of v3, /device:TPU:160, one launch (start us, length us, event | category | flops | bytes accessed | tf_op | source)
XLA Modules:
  0.0 84.9 jit_solution(16207366539731252056)
XLA Ops:
  1.9 81.1 %exchange.1 = (f32[2,768,1152]{2,1,0:T(8,128)S(1)}, bf16[768,1152]{1,0:T(8,128)(2,1)S(1)}, bf16[768,256]{1,0:T(8,128)(2,1)S(1)}, bf16[3072,1152]{1,0:T(8,128)(2,1)S(1)}, f32[8,128]{1,0:T(8,128)S(1)}) custom-call(bf16[768,1152]{1,0:T(8,128)(2,1)} %images.1, bf16[768,1152]{1,0:T(8,128)(2,1)} %texts.1, f32[1]{0:T(128)S(6)} %copy.6.scale_ref, f32[1]{0:T(128)S(6)} %copy.7.bias_ref), custom_call_target="tpu_custom_call" | custom-call | tf_op jit(solution)/shard_map/exchange/pallas_call | solution.py:180
  83.0 1.8 %finish.1 = (bf16[768,1152]{1,0:T(8,128)(2,1)}, bf16[768,1152]{1,0:T(8,128)(2,1)}) custom-call(f32[2,768,1152]{2,1,0:T(8,128)S(1)} %get-tuple-element.7.acc, bf16[768,1152]{1,0:T(8,128)(2,1)S(1)} %get-tuple-element.8.image_in, bf16[768,256]{1,0:T(8,128)(2,1)S(1)} %get-tuple-element.9.last_grad, bf16[3072,1152]{1,0:T(8,128)(2,1)S(1)} %get-tuple-element.10.got, ...), custom_call_target="tpu_custom_call" | custom-call | tf_op jit(solution)/shard_map/finish/pallas_call | solution.py:210

commit v4 on v3

--- a/solution.py
+++ b/solution.py
@@ -59,29 +59,35 @@
         )
 
     halves = (col >= n_col // 2, row >= n_row // 2)
+    lower = (jnp.logical_not(halves[0]), jnp.logical_not(halves[1]))
+    greeting = ((lower[0] | lower[1]), lower[1])
+    greeted = ((halves[0] | lower[1]), halves[1])
     barrier = pltpu.get_barrier_semaphore()
     for axis in range(2):
 
-        @pl.when(jnp.logical_not(halves[axis]))
+        @pl.when(greeting[axis])
         def _():
             pl.semaphore_signal(barrier, inc=1, device_id=partners[axis], device_id_type=MESH)
 
-    @pl.when(jnp.logical_or(halves[0], halves[1]))
-    def _():
-        pl.semaphore_wait(barrier, halves[0].astype(jnp.int32) + halves[1].astype(jnp.int32))
-
-    for axis in range(2):
-
-        @pl.when(halves[axis])
+    pl.semaphore_wait(barrier, greeted[0].astype(jnp.int32) + greeted[1].astype(jnp.int32))
+
+    for axis in range(2):
+
+        @pl.when(jnp.logical_not(greeting[axis]))
         def _():
             pl.semaphore_signal(
                 ready.at[axis], inc=1, device_id=partners[axis], device_id_type=MESH
             )
+
+    for axis in range(2):
+
+        @pl.when(greeted[axis])
+        def _():
             transfer(axis, 0).start()
 
     for axis in range(2):
 
-        @pl.when(jnp.logical_not(halves[axis]))
+        @pl.when(jnp.logical_not(greeted[axis]))
         def _():
             pl.semaphore_wait(ready.at[axis], 1)
             transfer(axis, 0).start()
@@ -123,7 +129,7 @@
                     @pl.when(index == 2 * start // BLOCK)
                     def _():
                         for axis in range(2):
-                            transfer(axis, number).wait()
+                            transfer(axis, number).wait_recv()
 
             at = pl.multiple_of((unit * per_unit + index) * BLOCK, BLOCK)
             block = got.at[pl.ds(at, BLOCK)]
@@ -138,7 +144,7 @@
     last = pl.ds(got.shape[0] - BLOCK, BLOCK)
     for number, columns in ((-2, pl.ds(0, LAST)), (-1, pl.ds(LAST, images.shape[1] - LAST))):
         for axis in range(2):
-            transfer(axis, len(plan) + number).wait()
+            transfer(axis, len(plan) + number).wait_recv()
         part = lax.dot_general(
             own[1, :, columns], got[last, columns], (((1,), (1,)), ((), ())),
             preferred_element_type=jnp.float32,
@@ -148,6 +154,10 @@
         else:
             value = jax.nn.sigmoid((logits[...] + part) * scale + bias)
             last_grad[...] = value.astype(jnp.bfloat16)
+
+    for number in range(len(plan)):
+        for axis in range(2):
+            transfer(axis, number).wait_send()
 
 
 def finish_kernel(acc, image_in, last_grad, got, scale_in, image_out, text_out, text, sem):

time: 86.5 us -> 86.5 us (level)
  no operation moved by 1% of the time
where the time goes in v4:
time: 86.5 us; the launch traced here: 84.9 us
  Pallas kernels  83 us (96%)
  between operations  1.93 us (2%)
    pallas_call x1, Pallas kernels, shards(): pl.pallas_call(exchange_kernel, out_shape=[pltpu.VMEM((2, rows, width), j...  81.1 us
    pallas_call x1, Pallas kernels, shards(): pl.pallas_call(finish_kernel, out_shape=[jax.ShapeDtypeStruct((rows, widt...  1.83 us

profile of v4, /device:TPU:160, one launch (start us, length us, event | category | flops | bytes accessed | tf_op | source)
XLA Modules:
  0.0 84.9 jit_solution(15401008552657400)
XLA Ops:
  1.9 81.1 %exchange.1 = (f32[2,768,1152]{2,1,0:T(8,128)S(1)}, bf16[768,1152]{1,0:T(8,128)(2,1)S(1)}, bf16[768,256]{1,0:T(8,128)(2,1)S(1)}, bf16[3072,1152]{1,0:T(8,128)(2,1)S(1)}, f32[8,128]{1,0:T(8,128)S(1)}) custom-call(bf16[768,1152]{1,0:T(8,128)(2,1)} %images.1, bf16[768,1152]{1,0:T(8,128)(2,1)} %texts.1, f32[1]{0:T(128)S(6)} %copy.6.scale_ref, f32[1]{0:T(128)S(6)} %copy.7.bias_ref), custom_call_target="tpu_custom_call" | custom-call | tf_op jit(solution)/shard_map/exchange/pallas_call | solution.py:190
  83.1 1.8 %finish.1 = (bf16[768,1152]{1,0:T(8,128)(2,1)}, bf16[768,1152]{1,0:T(8,128)(2,1)}) custom-call(f32[2,768,1152]{2,1,0:T(8,128)S(1)} %get-tuple-element.7.acc, bf16[768,1152]{1,0:T(8,128)(2,1)S(1)} %get-tuple-element.8.image_in, bf16[768,256]{1,0:T(8,128)(2,1)S(1)} %get-tuple-element.9.last_grad, bf16[3072,1152]{1,0:T(8,128)(2,1)S(1)} %get-tuple-element.10.got, ...), custom_call_target="tpu_custom_call" | custom-call | tf_op jit(solution)/shard_map/finish/pallas_call | solution.py:220
